TPU v7x, 256 devices: a whole 4x4x8 slice. The times are simulated.
256 devices in a mesh: dp: 8 (over x, core), ctx: 32 (over z, y).
Axes of the slice: x: 4, y: 4, z: 8, core: 2. Of those that a mesh axis runs over, the one named last changes fastest.
Arguments:
- queries: bfloat16 [65536, 256], P(('dp', 'ctx')), parts along dimension 0, may hold values from -6 to 6
- keys: bfloat16 [65536, 256], P(('dp', 'ctx')), parts along dimension 0, may hold values from -6 to 6
- values: bfloat16 [65536, 256], P(('dp', 'ctx')), parts along dimension 0, may hold values from -6 to 6
- document_ids: int32 [65536], P(('dp', 'ctx')), parts along dimension 0, may hold values from 0 to 3, never falling along the last dimension, each value on 1 to 4096 neighbouring positions
- output_weight: bfloat16 [256, 4096], P(None, 'ctx'), may hold values from -0.375 to 0.375
Outputs:
- projected: bfloat16 [65536, 4096], P(('dp', 'ctx')), parts along dimension 0
- log_normalizer: float32 [2, 65536], P(None, ('dp', 'ctx')), parts along dimension 1
There are 8 independent parts, one for each index of `dp`. A program takes and returns all parts, laid end to end along the dimension named above; an argument that names none is the same for every part. Nothing has to cross between parts.
Inputs may be any that keep to these rules, and one draw needn't show every extreme that they name: `document_ids`: document numbers never fall along the sequence; no document is longer than 4096 tokens, and one is exactly that long.
All inputs are finite; a program needn't handle non-finite values.
Results may differ from a plain program's by a relative error of at most 0.007.
Values may be sent and summed in bfloat16 or wider, within the bound.
A program may use at most 64 MiB of HBM per device.

v0:
```python
import math

import jax
import jax.numpy as jnp
from jax import lax
from jax.experimental import pallas as pl
from jax.experimental.pallas import tpu as pltpu
from jax.sharding import PartitionSpec as P

MESH = pl.DeviceIdType.MESH
HEADS = 2
HEAD_DIM = 128
NX, NC, NZ, NY = 4, 2, 8, 4
ROWS = 256
HALF = 128
FEATURES = HEADS * HEAD_DIM
MODEL = 4096
PARTS = NX * NC
PIECE = FEATURES // PARTS
REACH = 4
MASKED = -1e30
SCALE = 1.0 / math.sqrt(HEAD_DIM)
SCALE2 = SCALE * math.log2(math.e)
AROUND = [(0, 0), (0, 1), (1, 0)]
JUMP = 2


def attend_kernel(
    q_in, k_in, v_in, doc_in, w_in,
    att, w_all, lse_ref,
    q_all, k_all, vt_all, v_own, doc_q, doc_k, key_doc,
    acc, stat, o_send, o_recv, relay_k, relay_v, kept, kept_fade,
    loc_sem, kv_ss, kv_rs, a_ss, a_rs, one_ss, one_rs, o_ss, o_rs,
):
    dp = lax.axis_index("dp")
    ctx = lax.axis_index("ctx")
    x, core = dp // NC, lax.rem(dp, NC)
    z, y = ctx // NY, lax.rem(ctx, NY)

    def at(dx=0, flip=False, dz=0, dy=0):
        x_to = lax.rem(x + dx + NX, NX)
        core_to = 1 - core if flip else core
        z_to = lax.rem(z + dz + NZ, NZ)
        y_to = lax.rem(y + dy + NY, NY)
        return (x_to * NC + core_to, z_to * NY + y_to)

    def remote(src, dst, ss, rs, to):
        return pltpu.make_async_remote_copy(
            src_ref=src, dst_ref=dst, send_sem=ss, recv_sem=rs, device_id=to, device_id_type=MESH
        )

    barrier = pltpu.get_barrier_semaphore()
    partners = [at(dz=d) for d in range(1, NZ)]
    partners += [at(dy=d) for d in range(1, NY)]
    partners += [at(dx=d) for d in range(1, NX)]
    partners += [at(flip=True)]
    for to in partners:
        pl.semaphore_signal(barrier, inc=1, device_id=to, device_id_type=MESH)

    piece = pl.ds(pl.multiple_of(dp * PIECE, PIECE), PIECE)
    z_cols = pl.ds(pl.multiple_of(z * 128, 128), 128)
    locals_ = [
        pltpu.make_async_copy(k_in.at[:, 0:128], k_all.at[0, 0], loc_sem.at[0]),
        pltpu.make_async_copy(k_in.at[:, 128:256], k_all.at[0, 1], loc_sem.at[1]),
        pltpu.make_async_copy(doc_in, doc_q.at[0], loc_sem.at[2]),
        pltpu.make_async_copy(w_in.at[piece], w_all.at[0, piece, z_cols], loc_sem.at[3]),
        pltpu.make_async_copy(v_in, v_own, loc_sem.at[4]),
        pltpu.make_async_copy(q_in, q_all.at[0], loc_sem.at[5]),
    ]
    for copy in locals_:
        copy.start()

    def wait_bytes(like, sem):
        pltpu.make_async_copy(like, like, sem).wait()

    def kv_copy(h, k, part):
        ref = (k_all, vt_all)[part]
        return remote(
            ref.at[k, h], ref.at[k + 1, h],
            kv_ss.at[k], kv_rs.at[h, k, part], at(dz=1),
        )

    def advance(h, k, part):
        @pl.when(z >= k)
        def _():
            kv_copy(h, k - 1, part).wait_recv()

        last = REACH - 2 if (h, part) in AROUND else REACH - 1

        @pl.when((z >= k) & (z < NZ - 1) & (k <= last))
        def _():
            kv_copy(h, k, part).start()

    def around_out(h, part):
        return remote(
            (k_all, vt_all)[part].at[0, h], (relay_k, relay_v)[part].at[h],
            a_ss.at[0], a_rs.at[AROUND.index((h, part))], at(dz=-JUMP),
        )

    def around_in(h, part):
        return remote(
            (relay_k, relay_v)[part].at[h], (k_all, vt_all)[part].at[REACH, h],
            a_ss.at[1], kv_rs.at[h, REACH - 1, part], at(dz=-JUMP),
        )

    sends_around = z < NZ - REACH

    def send_around(index):
        @pl.when(sends_around)
        def _():
            around_out(*AROUND[index]).start()

    def relay_around(index, here):
        @pl.when(here)
        def _():
            around_out(*AROUND[index]).wait_recv()
            around_in(*AROUND[index]).start()

    relays_low = (z < NZ - REACH - JUMP) | (z == NZ - 1)
    relays_high = (z >= NZ - JUMP) & (z < NZ - 1)

    def group(index, pairs):
        return [remote(src, dst, one_ss.at[index], one_rs.at[index], to) for src, dst, to in pairs]

    q_copies = group(1 + 1, [(q_in, q_all.at[d], at(dy=d)) for d in range(1, NY)])
    dy_copies = group(3, [(doc_in, doc_q.at[d], at(dy=d)) for d in range(1, NY)])
    dz_copies = group(4, [(doc_in, doc_k.at[k - 1], at(dz=k)) for k in range(1, REACH + 1)])
    own_piece = w_all.at[0, piece, z_cols]
    w1_copies = group(5, [(own_piece, own_piece, at(dz=d)) for d in range(1, NZ)])
    own_column = w_all.at[0, piece]
    w2_copies = group(6, [(own_column, w_all.at[d, piece], at(dy=d)) for d in range(1, NY)])
    w3_first = group(7, [(own_column, own_column, at(dx=d)) for d in range(1, NX)])
    others = w_all.at[1:NY, piece]
    w3_rest = group(8, [(others, others, at(dx=d)) for d in (1, NX - 1)])
    far_part = lax.rem(x + NX // 2, NX) * NC + core
    far_rows = pl.ds(pl.multiple_of(far_part * PIECE, PIECE), PIECE)
    w2_far = group(0, [(w_all.at[0, far_rows], w_all.at[d, far_rows], at(dy=d)) for d in range(1, NY)])

    def part_rows(dx):
        part = lax.rem(x - dx + NX, NX) * NC + core
        return w_all.at[:, pl.ds(pl.multiple_of(part * PIECE, PIECE), PIECE)]

    w4_copies = group(9, [(part_rows(d), part_rows(d), at(flip=True)) for d in range(NX)])

    def weight_over_y():
        wait_bytes(w_all.at[0, 0 : (NZ - 1) * PIECE, 0:128], one_rs.at[5])
        for copy in w2_copies + w3_first:
            copy.start()

    def weight_over_x():
        wait_bytes(w_all.at[1:NY, piece], one_rs.at[6])
        for copy in w3_rest:
            copy.start()
        wait_bytes(w_all.at[1:NY, piece], one_rs.at[7])
        for copy in w2_far:
            copy.start()
        w4_copies[0].start()

    def weight_over_core():
        wait_bytes(w_all.at[1:NY, 0 : 2 * PIECE], one_rs.at[8])
        wait_bytes(w_all.at[1:NY, piece], one_rs.at[0])
        for d in range(1, NX):
            w4_copies[d].start()

    o_copies = [
        [
            remote(o_send.at[h, d - 1], o_recv.at[h, d - 1], o_ss.at[h], o_rs.at[h], at(dy=-d))
            for d in range(1, NY)
        ]
        for h in range(HEADS)
    ]

    def turned_docs(row):
        return jnp.broadcast_to(row, (128, ROWS)).T

    def half_weights(h, k, d, cols, causal):
        head = pl.ds(h * HEAD_DIM if isinstance(h, int) else pl.multiple_of(h * HEAD_DIM, HEAD_DIM), HEAD_DIM)
        scores = lax.dot_general(
            k_all[k, h], q_all[d, cols, head],
            (((1,), (1,)), ((), ())), preferred_element_type=jnp.float32,
        )
        visible = key_doc[k] == doc_q[d, :, cols]
        if causal:
            key_row = lax.broadcasted_iota(jnp.int32, (ROWS, HALF), 0)
            query_row = lax.broadcasted_iota(jnp.int32, (ROWS, HALF), 1) + cols.start
            visible = visible & (key_row <= query_row)
        scores = jnp.where(visible, scores, MASKED)
        old = stat[d, h, 0:1, cols]
        top = jnp.maximum(jnp.max(scores, axis=0, keepdims=True), old)
        weights = jnp.exp2((scores - top) * SCALE2)
        fade = jnp.exp2((old - top) * SCALE2)
        total = stat[d, h, 1:2, cols] * fade + jnp.sum(weights, axis=0, keepdims=True)
        stat[d, h, 1:2, cols] = total
        stat[d, h, 0:1, cols] = top
        return weights.astype(jnp.bfloat16), fade

    def half_sum(h, k, d, cols, weights, fade):
        product = jnp.dot(vt_all[k, h], weights, preferred_element_type=jnp.float32)
        acc[d, h, :, cols] = acc[d, h, :, cols] * fade + product

    halves = [slice(start, start + HALF) for start in range(0, ROWS, HALF)]

    def tile(h, k, d, causal=False):
        for cols in halves:
            half_sum(h, k, d, cols, *half_weights(h, k, d, cols, causal))

    def tile_weights(h, k, d):
        for cols in halves:
            kept[d, :, cols], kept_fade[d, 0:1, cols] = half_weights(h, k, d, cols, False)

    def tile_sum(h, k, d):
        for cols in halves:
            half_sum(h, k, d, cols, kept[d, :, cols], kept_fade[d, 0:1, cols])

    def thirds(row):
        high = row.astype(jnp.bfloat16).astype(jnp.float32)
        rest = row - high
        middle = rest.astype(jnp.bfloat16).astype(jnp.float32)
        return [high, middle, rest - middle]

    def give_back(h, d):
        rows = thirds(stat[d, h, 0:1]) + thirds(stat[d, h, 1:2])
        rows += [jnp.zeros((16 - len(rows), ROWS), jnp.float32)]
        o_send[h, d - 1, 0:HEAD_DIM] = acc[d, h].astype(jnp.bfloat16)
        o_send[h, d - 1, HEAD_DIM : HEAD_DIM + 16] = jnp.concatenate(rows, axis=0).astype(jnp.bfloat16)
        o_copies[h][d - 1].start()

    locals_[0].wait()
    locals_[1].wait()
    pl.semaphore_wait(barrier, len(partners))

    def send_own(h, part):
        @pl.when(z < NZ - 1)
        def _():
            kv_copy(h, 0, part).start()

    send_own(0, 0)
    send_around(0)
    for copy in dz_copies + dy_copies:
        copy.start()
    locals_[3].wait()
    locals_[4].wait()
    v_turned = v_own[...].T
    for h in range(HEADS):
        vt_all[0, h] = v_turned[h * HEAD_DIM : (h + 1) * HEAD_DIM]
    send_own(0, 1)
    for copy in q_copies:
        copy.start()
    send_own(1, 1)
    for copy in w1_copies:
        copy.start()
    send_around(1)

    locals_[2].wait()
    locals_[5].wait()
    acc[...] = jnp.zeros_like(acc)
    stat[:, :, 0:1] = jnp.full((NY, HEADS, 1, ROWS), MASKED, jnp.float32)
    stat[:, :, 1:2] = jnp.zeros((NY, HEADS, 1, ROWS), jnp.float32)
    key_doc[0] = turned_docs(doc_q[0])
    for h in range(HEADS):
        tile(h, 0, 0, causal=True)

    advance(0, 1, 0)
    advance(0, 1, 1)
    send_own(1, 0)
    send_around(2)
    wait_bytes(doc_k, one_rs.at[4])
    for k in range(1, REACH + 1):
        @pl.when(z >= k)
        def _(k=k):
            key_doc[k] = turned_docs(doc_k[k - 1])
    weight_over_y()
    relay_around(0, relays_low)
    advance(0, 2, 0)
    advance(1, 1, 1)
    relay_around(1, relays_low)
    wait_bytes(q_all.at[1:NY], one_rs.at[2])
    wait_bytes(doc_q.at[1:NY], one_rs.at[3])

    for low in range(NY - 1):
        @pl.when(y == low)
        def _(low=low):
            for d in range(low + 1, NY):
                for h in range(HEADS):
                    tile(h, 0, d)

    def give_back_early(h):
        for d in range(NY - 1, 0, -1):
            @pl.when(y < d)
            def _(d=d):
                give_back(h, d)

    def far(h, step):
        for high in range(1, NY):
            @pl.when((z >= REACH) & (y == high))
            def _(high=high):
                for d in range(1, high + 1):
                    step(h, REACH, d)

    def give_back_late(h):
        for d in range(NY - 1, 0, -1):
            @pl.when(y >= d)
            def _(d=d):
                give_back(h, d)

    def far_own(h):
        @pl.when(z >= REACH)
        def _():
            tile(h, REACH, 0)

    arrivals = [
        [(0, 2, 1), (1, 1, 0)],
        [],
        [(1, 2, 1)],
        [(0, 3, 0), (0, 3, 1)],
        [(1, 2, 0)],
        [(1, 3, 1)],
    ]

    def unit(u, carry):
        for index, chunks in enumerate(arrivals):
            @pl.when(u == index)
            def _(index=index, chunks=chunks):
                if index == 2:
                    weight_over_x()
                    for chunk in range(len(AROUND)):
                        relay_around(chunk, relays_high)
                for chunk in chunks:
                    advance(*chunk)
                if index == 0:
                    relay_around(2, relays_low)
                if index == 4:
                    give_back_early(0)
                if index == 5:
                    advance(0, REACH, 0)
                    advance(0, REACH, 1)
                    far(0, tile)
                    give_back_late(0)
                    advance(1, 3, 0)

        past = [0, (u + 4) // 5, (u + 3) // 5, u // 3, u // 4, u // 5]
        h = past[2] - past[3] + past[4]
        k = 1 + past[1] - past[2] + 2 * past[3] - past[4] + past[5]

        @pl.when(z >= k)
        def _():
            for d in range(NY):
                tile(h, k, d)

        return carry

    lax.fori_loop(0, len(arrivals), unit, 0)
    give_back_early(1)

    advance(1, REACH, 0)
    far(1, tile_weights)
    advance(1, REACH, 1)
    for d in range(NY - 1, 0, -1):
        @pl.when((z >= REACH) & (y >= d))
        def _(d=d):
            tile_sum(1, REACH, d)

        @pl.when(y >= d)
        def _(d=d):
            give_back(1, d)
    far_own(0)
    far_own(1)
    weight_over_core()

    for h in range(HEADS):
        wait_bytes(o_recv.at[h], o_rs.at[h])
        tops, sums = [stat[0, h, 0:1]], [stat[0, h, 1:2]]
        for d in range(NY - 1):
            rows = o_recv[h, d, HEAD_DIM : HEAD_DIM + 16].astype(jnp.float32)
            tops.append(rows[0:1] + rows[1:2] + rows[2:3])
            sums.append(rows[3:4] + rows[4:5] + rows[5:6])
        top = tops[0]
        for other in tops[1:]:
            top = jnp.maximum(top, other)
        shares = [jnp.exp2((one - top) * SCALE2) for one in tops]
        total = sums[0] * shares[0]
        for d in range(1, NY):
            total = total + sums[d] * shares[d]
        lse_ref[h : h + 1] = top * SCALE + jnp.log(total)
        value = acc[0, h] * (shares[0] / total)
        for d in range(1, NY):
            value = value + o_recv[h, d - 1, 0:HEAD_DIM].astype(jnp.float32) * (shares[d] / total)
        att[:, h * HEAD_DIM : (h + 1) * HEAD_DIM] = value.T.astype(jnp.bfloat16)

    wait_bytes(w_all.at[:, 0 : NX * PIECE], one_rs.at[9])

    for k in range(REACH):
        @pl.when((z >= k) & (z < NZ - 1))
        def _(k=k):
            wait_bytes(k_all.at[0:2] if k < REACH - 1 else k_all.at[0, 0], kv_ss.at[k])

    @pl.when(sends_around)
    def _():
        wait_bytes(k_all.at[0:3, 0], a_ss.at[0])

    @pl.when(relays_low | relays_high)
    def _():
        wait_bytes(k_all.at[0:3, 0], a_ss.at[1])

    wait_bytes(q_all.at[1:NY], one_ss.at[2])
    wait_bytes(doc_q.at[1:NY], one_ss.at[3])
    wait_bytes(doc_k, one_ss.at[4])
    wait_bytes(w_all.at[0, 0 : (NZ - 1) * PIECE, 0:128], one_ss.at[5])
    wait_bytes(w_all.at[1:NY, piece], one_ss.at[6])
    wait_bytes(w_all.at[1:NY, piece], one_ss.at[7])
    wait_bytes(w_all.at[1:NY, 0 : 2 * PIECE], one_ss.at[8])
    wait_bytes(w_all.at[1:NY, piece], one_ss.at[0])
    wait_bytes(w_all.at[:, 0 : NX * PIECE], one_ss.at[9])
    for h in range(HEADS):
        wait_bytes(o_send.at[h], o_ss.at[h])


def project_kernel(att, w_all, lse_in, out_ref, lse_ref, stage, sems):
    lse_copy = pltpu.make_async_copy(lse_in, lse_ref, sems.at[NZ])
    lse_copy.start()
    attended = att[...]
    y = lax.rem(lax.axis_index("ctx"), NY)
    writes = []
    width = NY * 128
    for block in range(NZ):
        weight = jnp.concatenate(
            [w_all[lax.rem(y - c + NY, NY), :, block * 128 : (block + 1) * 128] for c in range(NY)], axis=1
        )
        cols = slice(block * width, (block + 1) * width)
        stage[:, cols] = jnp.dot(
            attended, weight, preferred_element_type=jnp.float32
        ).astype(jnp.bfloat16)
        write = pltpu.make_async_copy(stage.at[:, cols], out_ref.at[:, cols], sems.at[block])
        write.start()
        writes.append(write)
    for write in writes + [lse_copy]:
        write.wait()


def on_device(queries, keys, values, document_ids, output_weight):
    bf16, f32, i32 = jnp.bfloat16, jnp.float32, jnp.int32
    dma = pltpu.SemaphoreType.DMA
    anywhere = pl.BlockSpec(memory_space=pl.ANY)
    local = pl.BlockSpec(memory_space=pltpu.VMEM)
    attended, weight, lse = pl.pallas_call(
        attend_kernel,
        out_shape=(
            jax.ShapeDtypeStruct((ROWS, FEATURES), bf16),
            jax.ShapeDtypeStruct((NY, FEATURES, NZ * 128), bf16),
            jax.ShapeDtypeStruct((HEADS, ROWS), f32),
        ),
        in_specs=[pl.BlockSpec(memory_space=pltpu.HBM)] * 5,
        out_specs=(local, anywhere, local),
        scratch_shapes=[
            pltpu.VMEM((NY, ROWS, FEATURES), bf16),
            pltpu.VMEM((REACH + 1, HEADS, ROWS, HEAD_DIM), bf16),
            pltpu.VMEM((REACH + 1, HEADS, HEAD_DIM, ROWS), bf16),
            pltpu.VMEM((ROWS, FEATURES), bf16),
            pltpu.VMEM((NY, 1, ROWS), i32),
            pltpu.VMEM((REACH, 1, ROWS), i32),
            pltpu.VMEM((REACH + 1, ROWS, 128), i32),
            pltpu.VMEM((NY, HEADS, HEAD_DIM, ROWS), f32),
            pltpu.VMEM((NY, HEADS, 2, ROWS), f32),
            pltpu.VMEM((HEADS, NY - 1, HEAD_DIM + 16, ROWS), bf16),
            pltpu.VMEM((HEADS, NY - 1, HEAD_DIM + 16, ROWS), bf16),
            pltpu.VMEM((HEADS, ROWS, HEAD_DIM), bf16),
            pltpu.VMEM((HEADS, HEAD_DIM, ROWS), bf16),
            pltpu.VMEM((NY, ROWS, ROWS), bf16),
            pltpu.VMEM((NY, 1, ROWS), f32),
            dma((6,)), dma((REACH,)), dma((HEADS, REACH, 2)), dma((2,)), dma((3,)),
            dma((10,)), dma((10,)), dma((HEADS,)), dma((HEADS,)),
        ],
        compiler_params=pltpu.CompilerParams(
            collective_id=0, has_side_effects=True, vmem_limit_bytes=32 << 20
        ),
    )(*[
        pltpu.with_memory_space_constraint(one, pltpu.HBM)
        for one in (queries, keys, values, document_ids.reshape(1, ROWS), output_weight)
    ])
    return pl.pallas_call(
        project_kernel,
        out_shape=(
            jax.ShapeDtypeStruct((ROWS, MODEL), bf16),
            jax.ShapeDtypeStruct((HEADS, ROWS), f32),
        ),
        in_specs=[local, local, anywhere],
        out_specs=(anywhere, anywhere),
        scratch_shapes=[pltpu.VMEM((ROWS, MODEL), bf16), dma((NZ + 1,))],
        compiler_params=pltpu.CompilerParams(vmem_limit_bytes=32 << 20),
    )(attended, weight, lse)


def solution(mesh):
    in_specs = (
        P(("dp", "ctx"), None),
        P(("dp", "ctx"), None),
        P(("dp", "ctx"), None),
        P(("dp", "ctx")),
        P(None, "ctx"),
    )
    out_specs = (P(("dp", "ctx"), None), P(None, ("dp", "ctx")))
    return jax.shard_map(
        on_device, mesh=mesh, in_specs=in_specs, out_specs=out_specs, check_vma=False
    )
```

profile of v0, /device:TPU:128, one launch (start us, length us, event | category | flops | bytes accessed | tf_op | source)
XLA Modules:
  0.0 36.5 jit_solution(11130122302135562274)
XLA Ops:
  0.6 34.2 %shard_map.68 = (bf16[256,256]{1,0:T(8,128)(2,1)S(1)}, bf16[4,256,1024]{2,1,0:T(8,128)(2,1)S(1)}, f32[2,256]{1,0:T(2,128)S(1)}) custom-call(bf16[256,256]{1,0:T(8,128)(2,1)} %q_in.1, bf16[256,256]{1,0:T(8,128)(2,1)} %k_in.1, bf16[256,256]{1,0:T(8,128)(2,1)} %v_in.1, s32[1,256]{1,0:T(1,128)} %bitcast.1, bf16[256,128]{1,0:T(8,128)(2,1)} %w_in.1), custom_call_target="tpu_custom_call" | custom-call | tf_op jit(solution)/shard_map/pallas_call | solution.py:445
  34.8 1.7 %shard_map.69 = (bf16[256,4096]{1,0:T(8,128)(2,1)}, f32[2,256]{1,0:T(2,128)}) custom-call(bf16[256,256]{1,0:T(8,128)(2,1)S(1)} %get-tuple-element.5.att, bf16[4,256,1024]{2,1,0:T(8,128)(2,1)S(1)} %get-tuple-element.6.w_all, f32[2,256]{1,0:T(2,128)S(1)} %get-tuple-element.7.lse_in), custom_call_target="tpu_custom_call" | custom-call | tf_op jit(solution)/shard_map/pallas_call | solution.py:480
where the time goes:
time: 36.6 us; the launch traced here: 36.5 us
  Pallas kernels  35.9 us (98%)
  between operations  0.64 us (2%)
    pallas_call x1, Pallas kernels, on_device(): pl.pallas_call(attend_kernel, out_shape=(jax.ShapeDtypeStruct((ROWS, FEAT...  34.2 us
    pallas_call x1, Pallas kernels, on_device(): pl.pallas_call(project_kernel, out_shape=(jax.ShapeDtypeStruct((ROWS, MOD...  1.7 us

commit v1 on v0

--- a/solution.py
+++ b/solution.py
@@ -269,10 +269,10 @@
         @pl.when(z >= k)
         def _(k=k):
             key_doc[k] = turned_docs(doc_k[k - 1])
-    weight_over_y()
     relay_around(0, relays_low)
     advance(0, 2, 0)
     advance(1, 1, 1)
+    weight_over_y()
     relay_around(1, relays_low)
     wait_bytes(q_all.at[1:NY], one_rs.at[2])
     wait_bytes(doc_q.at[1:NY], one_rs.at[3])
@@ -314,7 +314,6 @@
         [(1, 2, 1)],
         [(0, 3, 0), (0, 3, 1)],
         [(1, 2, 0)],
-        [(1, 3, 1)],
     ]
 
     def unit(u, carry):
@@ -331,12 +330,6 @@
                     relay_around(2, relays_low)
                 if index == 4:
                     give_back_early(0)
-                if index == 5:
-                    advance(0, REACH, 0)
-                    advance(0, REACH, 1)
-                    far(0, tile)
-                    give_back_late(0)
-                    advance(1, 3, 0)
 
         past = [0, (u + 4) // 5, (u + 3) // 5, u // 3, u // 4, u // 5]
         h = past[2] - past[3] + past[4]
@@ -350,7 +343,21 @@
         return carry
 
     lax.fori_loop(0, len(arrivals), unit, 0)
-    give_back_early(1)
+    advance(1, 3, 1)
+    advance(0, REACH, 0)
+    advance(0, REACH, 1)
+    far(0, tile)
+    give_back_late(0)
+    advance(1, 3, 0)
+
+    def near_last(first):
+        for high in range(NY):
+            @pl.when((z >= REACH - 1) & (y == high))
+            def _(high=high):
+                for d in range(1, high + 1) if first else [0, *range(high + 1, NY)]:
+                    tile(1, REACH - 1, d)
+
+    near_last(True)
 
     advance(1, REACH, 0)
     far(1, tile_weights)
@@ -363,6 +370,8 @@
         @pl.when(y >= d)
         def _(d=d):
             give_back(1, d)
+    near_last(False)
+    give_back_early(1)
     far_own(0)
     far_own(1)
     weight_over_core()

time: 36.6 us -> 36.5 us (level)
  no operation moved by 1% of the time
where the time goes in v1:
time: 36.5 us; the launch traced here: 36.4 us
  Pallas kernels  35.8 us (98%)
  between operations  0.64 us (2%)
    pallas_call x1, Pallas kernels, on_device(): pl.pallas_call(attend_kernel, out_shape=(jax.ShapeDtypeStruct((ROWS, FEAT...  34.1 us
    pallas_call x1, Pallas kernels, on_device(): pl.pallas_call(project_kernel, out_shape=(jax.ShapeDtypeStruct((ROWS, MOD...  1.7 us

profile of v1, /device:TPU:128, one launch (start us, length us, event | category | flops | bytes accessed | tf_op | source)
XLA Modules:
  0.0 36.4 jit_solution(5970087306934064200)
XLA Ops:
  0.6 34.1 %shard_map.68 = (bf16[256,256]{1,0:T(8,128)(2,1)S(1)}, bf16[4,256,1024]{2,1,0:T(8,128)(2,1)S(1)}, f32[2,256]{1,0:T(2,128)S(1)}) custom-call(bf16[256,256]{1,0:T(8,128)(2,1)} %q_in.1, bf16[256,256]{1,0:T(8,128)(2,1)} %k_in.1, bf16[256,256]{1,0:T(8,128)(2,1)} %v_in.1, s32[1,256]{1,0:T(1,128)} %bitcast.1, bf16[256,128]{1,0:T(8,128)(2,1)} %w_in.1), custom_call_target="tpu_custom_call" | custom-call | tf_op jit(solution)/shard_map/pallas_call | solution.py:454
  34.7 1.7 %shard_map.69 = (bf16[256,4096]{1,0:T(8,128)(2,1)}, f32[2,256]{1,0:T(2,128)}) custom-call(bf16[256,256]{1,0:T(8,128)(2,1)S(1)} %get-tuple-element.5.att, bf16[4,256,1024]{2,1,0:T(8,128)(2,1)S(1)} %get-tuple-element.6.w_all, f32[2,256]{1,0:T(2,128)S(1)} %get-tuple-element.7.lse_in), custom_call_target="tpu_custom_call" | custom-call | tf_op jit(solution)/shard_map/pallas_call | solution.py:489

commit v2 on v1

--- a/solution.py
+++ b/solution.py
@@ -158,9 +158,10 @@
 
     def weight_over_core():
         wait_bytes(w_all.at[1:NY, 0 : 2 * PIECE], one_rs.at[8])
+        for d in (1, NX - 1):
+            w4_copies[d].start()
         wait_bytes(w_all.at[1:NY, piece], one_rs.at[0])
-        for d in range(1, NX):
-            w4_copies[d].start()
+        w4_copies[NX // 2].start()
 
     o_copies = [
         [
@@ -244,8 +245,8 @@
     for h in range(HEADS):
         vt_all[0, h] = v_turned[h * HEAD_DIM : (h + 1) * HEAD_DIM]
     send_own(0, 1)
-    for copy in q_copies:
-        copy.start()
+    for d in (2, 1, 3):
+        q_copies[d - 1].start()
     send_own(1, 1)
     for copy in w1_copies:
         copy.start()
@@ -394,7 +395,7 @@
         value = acc[0, h] * (shares[0] / total)
         for d in range(1, NY):
             value = value + o_recv[h, d - 1, 0:HEAD_DIM].astype(jnp.float32) * (shares[d] / total)
-        att[:, h * HEAD_DIM : (h + 1) * HEAD_DIM] = value.T.astype(jnp.bfloat16)
+        att[:, h * HEAD_DIM : (h + 1) * HEAD_DIM] = value.astype(jnp.bfloat16).T
 
     wait_bytes(w_all.at[:, 0 : NX * PIECE], one_rs.at[9])
 

time: 36.5 us -> 36.5 us (level)
  no operation moved by 1% of the time
where the time goes in v2:
time: 36.5 us; the launch traced here: 36.4 us
  Pallas kernels  35.8 us (98%)
  between operations  0.64 us (2%)
    pallas_call x1, Pallas kernels, on_device(): pl.pallas_call(attend_kernel, out_shape=(jax.ShapeDtypeStruct((ROWS, FEAT...  34.1 us
    pallas_call x1, Pallas kernels, on_device(): pl.pallas_call(project_kernel, out_shape=(jax.ShapeDtypeStruct((ROWS, MOD...  1.7 us

profile of v2, /device:TPU:128, one launch (start us, length us, event | category | flops | bytes accessed | tf_op | source)
XLA Modules:
  0.0 36.4 jit_solution(15858082870132674122)
XLA Ops:
  0.6 34.1 %shard_map.68 = (bf16[256,256]{1,0:T(8,128)(2,1)S(1)}, bf16[4,256,1024]{2,1,0:T(8,128)(2,1)S(1)}, f32[2,256]{1,0:T(2,128)S(1)}) custom-call(bf16[256,256]{1,0:T(8,128)(2,1)} %q_in.1, bf16[256,256]{1,0:T(8,128)(2,1)} %k_in.1, bf16[256,256]{1,0:T(8,128)(2,1)} %v_in.1, s32[1,256]{1,0:T(1,128)} %bitcast.1, bf16[256,128]{1,0:T(8,128)(2,1)} %w_in.1), custom_call_target="tpu_custom_call" | custom-call | tf_op jit(solution)/shard_map/pallas_call | solution.py:455
  34.7 1.7 %shard_map.69 = (bf16[256,4096]{1,0:T(8,128)(2,1)}, f32[2,256]{1,0:T(2,128)}) custom-call(bf16[256,256]{1,0:T(8,128)(2,1)S(1)} %get-tuple-element.5.att, bf16[4,256,1024]{2,1,0:T(8,128)(2,1)S(1)} %get-tuple-element.6.w_all, f32[2,256]{1,0:T(2,128)S(1)} %get-tuple-element.7.lse_in), custom_call_target="tpu_custom_call" | custom-call | tf_op jit(solution)/shard_map/pallas_call | solution.py:490

commit v3 on v2

--- a/solution.py
+++ b/solution.py
@@ -85,9 +85,10 @@
         def _():
             kv_copy(h, k - 1, part).wait_recv()
 
-        last = REACH - 2 if (h, part) in AROUND else REACH - 1
-
-        @pl.when((z >= k) & (z < NZ - 1) & (k <= last))
+        if k > (REACH - 2 if (h, part) in AROUND else REACH - 1):
+            return
+
+        @pl.when((z >= k) & (z < NZ - 1))
         def _():
             kv_copy(h, k, part).start()
 

time: 36.5 us -> 36.5 us (level)
  no operation moved by 1% of the time
where the time goes in v3:
time: 36.5 us; the launch traced here: 36.4 us
  Pallas kernels  35.8 us (98%)
  between operations  0.64 us (2%)
    pallas_call x1, Pallas kernels, on_device(): pl.pallas_call(attend_kernel, out_shape=(jax.ShapeDtypeStruct((ROWS, FEAT...  34.1 us
    pallas_call x1, Pallas kernels, on_device(): pl.pallas_call(project_kernel, out_shape=(jax.ShapeDtypeStruct((ROWS, MOD...  1.7 us

profile of v3, /device:TPU:128, one launch (start us, length us, event | category | flops | bytes accessed | tf_op | source)
XLA Modules:
  0.0 36.4 jit_solution(15858082870132674122)
XLA Ops:
  0.6 34.1 %shard_map.68 = (bf16[256,256]{1,0:T(8,128)(2,1)S(1)}, bf16[4,256,1024]{2,1,0:T(8,128)(2,1)S(1)}, f32[2,256]{1,0:T(2,128)S(1)}) custom-call(bf16[256,256]{1,0:T(8,128)(2,1)} %q_in.1, bf16[256,256]{1,0:T(8,128)(2,1)} %k_in.1, bf16[256,256]{1,0:T(8,128)(2,1)} %v_in.1, s32[1,256]{1,0:T(1,128)} %bitcast.1, bf16[256,128]{1,0:T(8,128)(2,1)} %w_in.1), custom_call_target="tpu_custom_call" | custom-call | tf_op jit(solution)/shard_map/pallas_call | solution.py:456
  34.7 1.7 %shard_map.69 = (bf16[256,4096]{1,0:T(8,128)(2,1)}, f32[2,256]{1,0:T(2,128)}) custom-call(bf16[256,256]{1,0:T(8,128)(2,1)S(1)} %get-tuple-element.5.att, bf16[4,256,1024]{2,1,0:T(8,128)(2,1)S(1)} %get-tuple-element.6.w_all, f32[2,256]{1,0:T(2,128)S(1)} %get-tuple-element.7.lse_in), custom_call_target="tpu_custom_call" | custom-call | tf_op jit(solution)/shard_map/pallas_call | solution.py:491
